TPU v7x, 256 devices: a whole 4x4x8 slice. The times are simulated.
256 devices in a mesh: lon: 32 (over z, x), lat: 2 (over core), head: 4 (over y).
Axes of the slice: x: 4, y: 4, z: 8, core: 2. Of those that a mesh axis runs over, the one named last changes fastest.
Arguments:
- queries: bfloat16 [32, 1280, 1024], P('lat', 'lon', 'head'), may hold values from -49 to 49
- keys: bfloat16 [32, 1280, 1024], P('lat', 'lon', 'head'), may hold values from -49 to 49
- values: bfloat16 [32, 1280, 1024], P('lat', 'lon', 'head'), may hold values from -16 to 16
- grad_out: bfloat16 [32, 1280, 1024], P('lat', 'lon', 'head'), may hold values from -64 to 64
- key_mask: int32 [32, 1280], P('lat', 'lon'), may hold values from 0 to 1
- offsets: int32 [4, 160], P('lat', 'lon'), may hold values from -8 to 8, as said below
- regions: int32 [4, 160], P('lat', 'lon'), may hold values from 0 to 7
Outputs:
- grad_queries: bfloat16 [32, 1280, 1024], P('lat', 'lon', 'head')
- grad_keys: bfloat16 [32, 1280, 1024], P('lat', 'lon', 'head')
- grad_values: bfloat16 [32, 1280, 1024], P('lat', 'lon', 'head')
Inputs may be any that keep to these rules, and one draw needn't show every extreme that they name: `offsets`: some block has offset -8 and some block has offset 8.
All inputs are finite; a program needn't handle non-finite values.
Results may differ from a plain program's by a relative error of at most 0.0095.
Values may be sent and summed in bfloat16 or wider, within the bound.
A program may use at most 64 MiB of HBM per device.

v0:
```python
import jax
import jax.numpy as jnp
from jax import lax
from jax.sharding import PartitionSpec as P

HS = 64
WIN = 8
REG_DEV = 8
MASKED_SCORE = -1e30


def extended_2(cells, sides, width):
    for axis, dim in sides:
        count = lax.axis_size(axis)
        head = lax.slice_in_dim(cells, 0, width, axis=dim)
        tail = lax.slice_in_dim(cells, cells.shape[dim] - width, cells.shape[dim], axis=dim)
        cells = jnp.concatenate(
            [
                lax.ppermute(tail, axis, [(i, (i + 1) % count) for i in range(count)]),
                cells,
                lax.ppermute(head, axis, [((i + 1) % count, i) for i in range(count)]),
            ],
            axis=dim,
        )
    return cells


def split_heads(array, head_count):
    return array.reshape(array.shape[:-1] + (head_count, HS))


def to_blocks(array):
    lat_cells, lon_cells = (array.shape[0], array.shape[1])
    trailing = array.shape[2:]
    grid_blocks = array.reshape((lat_cells // WIN, WIN, lon_cells // WIN, WIN) + trailing)
    perm_axes = (0, 2, 1, 3) + tuple(range(4, grid_blocks.ndim))
    return grid_blocks.transpose(perm_axes).reshape(
        (lat_cells // WIN, lon_cells // WIN, WIN * WIN) + trailing
    )


def from_blocks(array):
    lat_blocks, lon_blocks = (array.shape[0], array.shape[1])
    trailing = array.shape[3:]
    grid_blocks = array.reshape((lat_blocks, lon_blocks, WIN, WIN) + trailing)
    perm_axes = (0, 2, 1, 3) + tuple(range(4, grid_blocks.ndim))
    return grid_blocks.transpose(perm_axes).reshape((lat_blocks * WIN, lon_blocks * WIN) + trailing)


def window_blocks(extended, along):
    lon_blocks = extended.shape[1] - 4
    return jnp.concatenate([extended[:, step : step + lon_blocks] for step in range(5)], axis=along)


def fold_blocks(grads):
    cells = WIN * WIN
    folded = None
    for step in range(5):
        piece = grads[:, :, step * cells : (step + 1) * cells]
        piece = jnp.pad(piece, ((0, 0), (step, 4 - step), (0, 0), (0, 0)))
        folded = piece if folded is None else folded + piece
    return folded


def local(queries, keys, values, grad_out, key_mask, offsets, regions):
    highest = lax.Precision.HIGHEST
    lat_cells, lon_cells, features = queries.shape
    head_count = features // HS
    logit_scale = HS ** (-0.5)
    rim_blocks = 2
    cell_count = lat_cells * lon_cells
    lat_blocks, lon_blocks = (lat_cells // WIN, lon_cells // WIN)
    key_blocks = to_blocks(keys)
    value_blocks = to_blocks(values)
    query_blocks = to_blocks(queries)
    cotan_blocks = to_blocks(grad_out)
    mask_blocks = to_blocks(key_mask)
    block_region = jnp.broadcast_to(
        regions[:, :, None], (lat_blocks, lon_blocks, WIN * WIN)
    ).reshape(cell_count)
    weights = (block_region[:, None] == jnp.arange(REG_DEV, dtype=jnp.int32)[None, :]).astype(
        jnp.float32
    )
    weights = weights * mask_blocks.reshape(cell_count).astype(jnp.float32)[:, None]
    divisor = jnp.maximum(jnp.sum(weights, axis=0), 1.0)
    weights_low = weights.astype(jnp.bfloat16).T
    pooled_k = jnp.dot(
        weights_low, key_blocks.reshape(cell_count, features), preferred_element_type=jnp.float32
    )
    pooled_v = jnp.dot(
        weights_low, value_blocks.reshape(cell_count, features), preferred_element_type=jnp.float32
    )
    pooled = (jnp.stack([pooled_k, pooled_v], axis=1) / divisor[:, None, None]).astype(jnp.bfloat16)
    gathered = lax.all_gather(pooled, "lat", axis=0, tiled=True)
    reg_count = gathered.shape[0]
    register_key_rows = gathered[:, 0].reshape(reg_count, head_count, HS)
    register_value_rows = gathered[:, 1].reshape(reg_count, head_count, HS)
    key_ext, value_ext, mask_ext = (
        extended_2(key_blocks, (("lon", 1),), rim_blocks),
        extended_2(value_blocks, (("lon", 1),), rim_blocks),
        extended_2(mask_blocks, (("lon", 1),), rim_blocks),
    )
    cand_k = split_heads(window_blocks(key_ext, 2), head_count)
    candidate_values = split_heads(window_blocks(value_ext, 2), head_count)
    cand_mask = window_blocks(mask_ext, 2)
    key_offset = (
        jnp.arange(5, dtype=jnp.int32)[:, None, None] * WIN
        - 2 * WIN
        + jnp.zeros((1, WIN, 1), jnp.int32)
        + jnp.arange(WIN, dtype=jnp.int32)[None, None, :]
    ).reshape(5 * WIN * WIN)
    window_start = offsets[:, :, None]
    usable = (
        (key_offset >= window_start - WIN)
        & (key_offset < window_start + 2 * WIN)
        & (cand_mask == 1)
    )
    usable_b = usable[:, :, None, None, :]
    query_block = split_heads(query_blocks, head_count)
    gradient_block = split_heads(cotan_blocks, head_count)
    score_win = (
        jnp.einsum("abqhd,abkhd->abhqk", query_block, cand_k, preferred_element_type=jnp.float32)
        * logit_scale
    )
    score_win = jnp.where(usable_b, score_win, MASKED_SCORE)
    register_scores = (
        jnp.einsum(
            "abqhd,khd->abhqk", query_block, register_key_rows, preferred_element_type=jnp.float32
        )
        * logit_scale
    )
    row_max = jnp.maximum(jnp.max(score_win, axis=-1), jnp.max(register_scores, axis=-1))
    exp_total = jnp.sum(jnp.where(usable_b, jnp.exp(score_win - row_max[..., None]), 0.0), axis=-1)
    exp_total = exp_total + jnp.sum(jnp.exp(register_scores - row_max[..., None]), axis=-1)
    log_total = row_max + jnp.log(exp_total)
    prob_win = jnp.where(usable_b, jnp.exp(score_win - log_total[..., None]), 0.0)
    prob_reg = jnp.exp(register_scores - log_total[..., None])
    window_lower_bound = prob_win.astype(jnp.bfloat16)
    register_lower_bound = prob_reg.astype(jnp.bfloat16)
    attended_output = jnp.einsum(
        "abhqk,abkhd->abqhd",
        window_lower_bound,
        candidate_values,
        preferred_element_type=jnp.float32,
    )
    attended_output = attended_output + jnp.einsum(
        "abhqk,khd->abqhd",
        register_lower_bound,
        register_value_rows,
        preferred_element_type=jnp.float32,
    )
    delta_dot = jnp.sum(gradient_block.astype(jnp.float32) * attended_output, axis=-1)
    delta_heads = delta_dot.transpose(0, 1, 3, 2)
    dprob_win = jnp.einsum(
        "abqhd,abkhd->abhqk", gradient_block, candidate_values, preferred_element_type=jnp.float32
    )
    register_prob_gradient = jnp.einsum(
        "abqhd,khd->abhqk", gradient_block, register_value_rows, preferred_element_type=jnp.float32
    )
    dscore_win = (prob_win * (dprob_win - delta_heads[..., None])).astype(jnp.bfloat16)
    register_score_gradient = (prob_reg * (register_prob_gradient - delta_heads[..., None])).astype(
        jnp.bfloat16
    )
    grad_q = logit_scale * (
        jnp.einsum("abhqk,abkhd->abqhd", dscore_win, cand_k, preferred_element_type=jnp.float32)
        + jnp.einsum(
            "abhqk,khd->abqhd",
            register_score_gradient,
            register_key_rows,
            preferred_element_type=jnp.float32,
        )
    )
    grad_queries = from_blocks(grad_q.reshape(lat_blocks, lon_blocks, WIN * WIN, features)).astype(
        jnp.bfloat16
    )
    reg_grad_k = logit_scale * jnp.einsum(
        "abhqk,abqhd->khd", register_score_gradient, query_block, preferred_element_type=jnp.float32
    )
    reg_grad_v = jnp.einsum(
        "abhqk,abqhd->khd", register_lower_bound, gradient_block, preferred_element_type=jnp.float32
    )
    reg_grads = jnp.stack(
        [reg_grad_k.reshape(reg_count, features), reg_grad_v.reshape(reg_count, features)], axis=1
    )
    own_grads = lax.psum_scatter(
        reg_grads.astype(jnp.bfloat16), "lat", scatter_dimension=0, tiled=True
    ).astype(jnp.float32)
    spread = jnp.dot(
        weights,
        (own_grads / divisor[:, None, None]).reshape(REG_DEV, 2 * features),
        precision=highest,
    )
    spread = spread.reshape(lat_blocks, lon_blocks, WIN * WIN, 2 * features)
    grad_kc = logit_scale * jnp.einsum(
        "abhqk,abqhd->abkhd", dscore_win, query_block, preferred_element_type=jnp.float32
    )
    grad_vc = jnp.einsum(
        "abhqk,abqhd->abkhd", window_lower_bound, gradient_block, preferred_element_type=jnp.float32
    )
    ext_k = fold_blocks(grad_kc.reshape(grad_kc.shape[:3] + (features,)))
    ext_v = fold_blocks(grad_vc.reshape(grad_vc.shape[:3] + (features,)))
    edges_k = jnp.concatenate([ext_k[:, :rim_blocks], ext_k[:, -rim_blocks:]], axis=1)
    edges_v = jnp.concatenate([ext_v[:, :rim_blocks], ext_v[:, -rim_blocks:]], axis=1)
    got_k, got_v = (
        extended_2(edges_k, (("lon", 1),), rim_blocks),
        extended_2(edges_v, (("lon", 1),), rim_blocks),
    )
    win_k = ext_k[:, rim_blocks:-rim_blocks].at[:, :rim_blocks].add(got_k[:, :rim_blocks])
    win_k = win_k.at[:, -rim_blocks:].add(got_k[:, -rim_blocks:])
    win_v = ext_v[:, rim_blocks:-rim_blocks].at[:, :rim_blocks].add(got_v[:, :rim_blocks])
    win_v = win_v.at[:, -rim_blocks:].add(got_v[:, -rim_blocks:])
    grad_keys = from_blocks((win_k + spread[..., :features]).astype(jnp.bfloat16))
    grad_values = from_blocks((win_v + spread[..., features:]).astype(jnp.bfloat16))
    return (grad_queries, grad_keys, grad_values)


def solution(mesh):
    in_specs = (
        P("lat", "lon", "head"),
        P("lat", "lon", "head"),
        P("lat", "lon", "head"),
        P("lat", "lon", "head"),
        P("lat", "lon"),
        P("lat", "lon"),
        P("lat", "lon"),
    )
    out_specs = (P("lat", "lon", "head"), P("lat", "lon", "head"), P("lat", "lon", "head"))
    return jax.shard_map(local, mesh=mesh, in_specs=in_specs, out_specs=out_specs, check_vma=False)
```

profile of v0, /device:TPU:1, one launch (start us, length us, event | category | flops | bytes accessed | tf_op | source)
XLA Modules:
  0.0 155.2 jit_solution(9662106261121816254)
XLA Ops:
  8.1 2.1 %collective-permute-start.2 = (s32[2,2,64]{2,0,1:T(2,128)S(1)}, s32[2,2,64]{2,0,1:T(2,128)S(1)}, u32[]{:S(2)}, u32[]{:S(2)}) collective-permute-start(s32[2,2,64]{2,0,1:T(2,128)S(1)} %get-tuple-element.97), channel_id=1, source_target_pairs={{0,8},{8,16},{16,24},{24,32},{32,40},{40,48},{48,56},{56,64},{64,7... | collective-permute-start | bytes 3080 | tf_op jit(solution)/shard_map/ppermute | solution.py:19
  10.3 6.6 %collective-permute-start.3 = (s32[2,2,64]{2,0,1:T(2,128)S(1)}, s32[2,2,64]{2,0,1:T(2,128)S(1)}, u32[]{:S(2)}, u32[]{:S(2)}) collective-permute-start(s32[2,2,64]{2,0,1:T(2,128)S(1)} %get-tuple-element.96), channel_id=1, source_target_pairs={{8,0},{16,8},{24,16},{32,24},{40,32},{48,40},{56,48},{64,56},{72,6... | collective-permute-start | bytes 3080 | tf_op jit(solution)/shard_map/ppermute | solution.py:21
  18.6 1.4 collective-permute-start.1
  21.8 4.7 %collective-permute-start.5 = (bf16[2,2,64,256]{3,2,1,0:T(8,128)(2,1)}, bf16[2,2,64,256]{3,2,1,0:T(8,128)(2,1)}, u32[]{:S(2)}, u32[]{:S(2)}) collective-permute-start(bf16[2,2,64,256]{3,2,1,0:T(8,128)(2,1)} %get-tuple-element.77), channel_id=1, source_target_pairs={{8,0},{16,8},{24,16},{32,24},{40,32},{48,40},{56,48},{64,56},{72,6... | collective-permute-start | bytes 393224 | tf_op jit(solution)/shard_map/ppermute | solution.py:21
  27.6 3.6 %all_gather.3 = bf16[16,2,256]{2,0,1:T(8,128)(2,1)S(1)} all-gather(bf16[8,2,256]{2,0,1:T(8,128)(2,1)S(1)} %fusion.51), channel_id=1, replica_groups=mesh['lon'=32,'lat'=2,'head'=4] {'lat'}, dimensions={0}, use_global_device_ids=true | all-gather | bytes 24576 | tf_op jit(solution)/shard_map/all_gather | solution.py:94
  32.0 1.1 copy.447
  35.4 1.2 copy.410
  36.6 1.2 copy.433
  37.8 1.1 copy.436
  39.2 1.1 pad_maximum_fusion.2
  40.3 1.1 copy.405
  41.4 1.1 copy.406
  43.6 1.1 copy.409
  44.7 4.1 %concatenate.77 = bf16[2,5,320,4,64]{2,4,3,1,0:T(8,128)(2,1)S(1)} concatenate(bf16[2,5,64,4,64]{2,4,3,1,0:T(8,128)(2,1)} %bitcast.189, bf16[2,5,64,4,64]{2,4,3,1,0:T(8,128)(2,1)} %bitcast.191, bf16[2,5,64,4,64]{2,4,3,1,0:T(8,128)(2,1)} %copy.410, bf16[2,5,64,4,64]{2,4,3,1,0:T(8,128)(2,1)} %bitcast.193, bf16[2,5,64,4,64]{2,4,3,1,0:T(8,128)(2,1)} %bitcast.195), dimensions={2} | concatenate | bytes 3276800 | tf_op jit(solution)/shard_map/concatenate | solution.py:52
  48.8 1.9 %bitcast_reduce_fusion = (f32[2,5,4,64]{3,2,1,0:T(4,128)S(1)}, f32[2,5,4,320,64]{3,4,2,1,0:T(8,128)S(1)}) fusion(pred[2,5,320]{2,1,0:T(8,128)(4,1)S(1)} %copy.416, bf16[2,5,64,4,64]{2,4,3,1,0:T(8,128)(2,1)} %copy.447, bf16[2,5,320,4,64]{2,4,3,1,0:T(8,128)(2,1)S(1)} %concatenate.77), kind=kOutput, calls=%fused_computation.4 | convolution fusion | flops 107312640 | bytes 5256320 | tf_op jit(solution)/shard_map/abqhd,abkhd->abhqk/dot_general | solution.py:122
  50.8 1.3 fusion.3
  52.8 2.1 %pad_maximum_fusion = (bf16[2,5,64,256]{3,2,1,0:T(8,128)(2,1)}, bf16[2,5,64,256]{3,2,1,0:T(8,128)(2,1)}, bf16[2,5,64,256]{3,2,1,0:T(8,128)(2,1)}, bf16[2,5,64,256]{3,2,1,0:T(8,128)(2,1)}) fusion(bf16[2,2,64,256]{3,2,1,0:T(8,128)(2,1)} %collective-permute-done.5, bf16[2,5,64,256]{3,2,1,0:T(8,128)(2,1)S(1)} %bitcast.184, ...), kind=kLoop, calls=%fused_computation.62 | loop fusion | flops 655360 | bytes 1900544 | tf_op jit(solution)/shard_map/concatenate | solution.py:17
  54.9 2.2 %copy.428 = bf16[2,5,64,256]{2,3,1,0:T(8,128)(2,1)} copy(bf16[2,5,64,256]{3,2,1,0:T(8,128)(2,1)} %get-tuple-element.75) | data formatting | bytes 655360 | tf_op jit(solution)/shard_map/slice | solution.py:52
  57.0 2.0 %copy.429 = bf16[2,5,64,256]{2,3,1,0:T(8,128)(2,1)} copy(bf16[2,5,64,256]{3,2,1,0:T(8,128)(2,1)} %get-tuple-element.76) | data formatting | bytes 655360 | tf_op jit(solution)/shard_map/slice | solution.py:52
  59.1 2.1 %copy.431 = bf16[2,5,64,256]{2,3,1,0:T(8,128)(2,1)} copy(bf16[2,5,64,256]{3,2,1,0:T(8,128)(2,1)} %get-tuple-element.68) | data formatting | bytes 655360 | tf_op jit(solution)/shard_map/slice | solution.py:52
  61.2 1.1 copy.432
  62.3 1.4 convolution_bitcast_fusion.3
  63.7 5.3 %concatenate.88 = bf16[2,5,320,4,64]{2,4,3,1,0:T(8,128)(2,1)} concatenate(bf16[2,5,64,4,64]{2,4,3,1,0:T(8,128)(2,1)} %bitcast.188, bf16[2,5,64,4,64]{2,4,3,1,0:T(8,128)(2,1)} %bitcast.190, bf16[2,5,64,4,64]{2,4,3,1,0:T(8,128)(2,1)} %copy.433, bf16[2,5,64,4,64]{2,4,3,1,0:T(8,128)(2,1)} %bitcast.192, bf16[2,5,64,4,64]{2,4,3,1,0:T(8,128)(2,1)} %bitcast.194), dimensions={2} | concatenate | bytes 3276800 | tf_op jit(solution)/shard_map/concatenate | solution.py:52
  69.0 4.5 %fusion.12 = f32[2,5,64,4]{2,3,1,0:T(4,128)S(1)} fusion(f32[2,5,64,4,64]{2,4,3,1,0:T(8,128)} %convolution_bitcast_fusion.3, bf16[2,5,320,4,64]{2,4,3,1,0:T(8,128)(2,1)} %concatenate.88, bf16[2,5,64,4,64]{2,4,3,1,0:T(8,128)(2,1)S(1)} %copy-done.27, f32[2,5,4,320,64]{3,4,2,1,0:T(8,128)} %copy-done, f32[2,5,4,64]{3,2,1,0:T(4,128)S(1)} %fusion.47, ...), kind=kOutput, calls=%fused_computation.22 | convolution fusion | flops 109606400 | bytes 5921920 | tf_op jit(solution)/shard_map/abhqk,abkhd->abqhd/dot_general | solution.py:140
  73.9 2.7 %fusion = bf16[2,5,4,64,320]{4,3,2,1,0:T(8,128)(2,1)} fusion(f32[2,5,4,320,64]{3,4,2,1,0:T(8,128)S(1)} %copy-done.1, bf16[2,5,64,4,64]{2,4,3,1,0:T(8,128)(2,1)S(1)} %copy-done.27, bf16[2,5,320,4,64]{2,4,3,1,0:T(8,128)(2,1)S(1)} %copy-done.28, f32[2,5,4,64]{3,2,1,0:T(4,128)S(1)} %bitcast.214, f32[2,5,4,64]{3,2,1,0:T(4,128)S(1)} %fusion.47, ...), kind=kOutput, calls=%fused_computation.1 | convolution fusion | flops 110592000 | bytes 6904960 | tf_op jit(solution)/shard_map/abqhd,abkhd->abhqk/dot_general | solution.py:154
  76.5 1.4 fusion.65
  77.9 3.6 %fusion.68 = (f32[2,5,64,256]{2,3,1,0:T(8,128)}, f32[2,5,64,256]{2,3,1,0:T(8,128)}, f32[2,5,64,256]{2,3,1,0:T(8,128)}, f32[2,5,64,256]{2,3,1,0:T(8,128)}, f32[2,5,64,256]{2,3,1,0:T(8,128)}) fusion(f32[2,5,320,256]{2,3,1,0:T(8,128)S(1)} %bitcast.181), kind=kLoop, calls=%fused_computation.132 | loop fusion | bytes 6553600 | tf_op jit(solution)/shard_map/slice | solution.py:59
  81.5 1.7 %copy.497 = f32[2,5,64,256]{3,2,1,0:T(8,128)S(1)} copy(f32[2,5,64,256]{2,3,1,0:T(8,128)} %get-tuple-element.55) | data formatting | bytes 1310720
  83.2 2.5 %copy.496 = f32[2,5,64,256]{3,2,1,0:T(8,128)} copy(f32[2,5,64,256]{2,3,1,0:T(8,128)} %get-tuple-element.52) | data formatting | bytes 1310720
  85.8 2.6 %copy.495 = f32[2,5,64,256]{3,2,1,0:T(8,128)} copy(f32[2,5,64,256]{2,3,1,0:T(8,128)} %get-tuple-element.53) | data formatting | bytes 1310720
  88.3 2.6 %copy.494 = f32[2,5,64,256]{3,2,1,0:T(8,128)} copy(f32[2,5,64,256]{2,3,1,0:T(8,128)} %get-tuple-element.54) | data formatting | bytes 1310720
  90.9 2.5 %copy.493 = f32[2,5,64,256]{3,2,1,0:T(8,128)} copy(f32[2,5,64,256]{2,3,1,0:T(8,128)} %get-tuple-element.51) | data formatting | bytes 1310720
  93.5 3.1 %pad_add_fusion = f32[2,9,64,256]{3,2,1,0:T(8,128)} fusion(f32[2,5,64,256]{3,2,1,0:T(8,128)S(1)} %copy.497, f32[2,5,64,256]{3,2,1,0:T(8,128)} %copy.496, f32[2,5,64,256]{3,2,1,0:T(8,128)} %copy.495, f32[2,5,64,256]{3,2,1,0:T(8,128)} %copy.494, f32[2,5,64,256]{3,2,1,0:T(8,128)} %copy.493), kind=kLoop, calls=%fused_computation.28 | loop fusion | flops 1179648 | bytes 4456448 | tf_op jit(solution)/shard_map/add | solution.py:61
  99.6 2.5 %convolution_multiply_fusion = f32[2,5,4,320,64]{3,4,2,1,0:T(8,128)} fusion(bf16[2,5,64,4,64]{2,4,3,1,0:T(8,128)(2,1)S(1)} %copy-done.23, bf16[2,5,4,64,320]{4,3,2,1,0:T(8,128)(2,1)S(1)} %copy-done.22), kind=kOutput, calls=%fused_computation.12 | convolution fusion | flops 105676800 | bytes 5242880 | tf_op jit(solution)/shard_map/abhqk,abqhd->abkhd/dot_general | solution.py:194
  102.1 1.7 %fusion.11 = bf16[2,5,64,4,64]{2,4,3,1,0:T(8,128)(2,1)} fusion(f32[2,5,64,4,64]{2,4,3,1,0:T(8,128)S(1)} %convolution_bitcast_fusion.2, bf16[2,5,320,4,64]{2,4,3,1,0:T(8,128)(2,1)S(1)} %concatenate.77, bf16[2,5,4,64,320]{4,3,2,1,0:T(8,128)(2,1)S(1)} %copy-done.22), kind=kOutput, calls=%fused_computation.21 | convolution fusion | flops 105349120 | bytes 4259840 | tf_op jit(solution)/shard_map/abhqk,abkhd->abqhd/dot_general | solution.py:165
  104.6 6.2 %fusion.69 = (f32[2,5,64,256]{2,3,1,0:T(8,128)}, f32[2,5,64,256]{2,3,1,0:T(8,128)S(1)}, f32[2,5,64,256]{2,3,1,0:T(8,128)}, f32[2,5,64,256]{2,3,1,0:T(8,128)}, f32[2,5,64,256]{2,3,1,0:T(8,128)}) fusion(f32[2,5,320,256]{2,3,1,0:T(8,128)} %bitcast.180), kind=kLoop, calls=%fused_computation.133 | loop fusion | bytes 6553600 | tf_op jit(solution)/shard_map/slice | solution.py:59
  110.8 1.7 %copy.492 = f32[2,5,64,256]{3,2,1,0:T(8,128)S(1)} copy(f32[2,5,64,256]{2,3,1,0:T(8,128)} %get-tuple-element.60) | data formatting | bytes 1310720
  112.9 1.9 %copy.490 = f32[2,5,64,256]{3,2,1,0:T(8,128)S(1)} copy(f32[2,5,64,256]{2,3,1,0:T(8,128)} %get-tuple-element.58) | data formatting | bytes 1310720
  114.8 1.9 %copy.489 = f32[2,5,64,256]{3,2,1,0:T(8,128)S(1)} copy(f32[2,5,64,256]{2,3,1,0:T(8,128)} %get-tuple-element.59) | data formatting | bytes 1310720
  116.8 2.8 %copy.488 = f32[2,5,64,256]{3,2,1,0:T(8,128)} copy(f32[2,5,64,256]{2,3,1,0:T(8,128)} %get-tuple-element.56) | data formatting | bytes 1310720
  119.6 2.4 %pad_add_fusion.1 = f32[2,9,64,256]{3,2,1,0:T(8,128)} fusion(f32[2,5,64,256]{3,2,1,0:T(8,128)S(1)} %copy.492, f32[2,5,64,256]{3,2,1,0:T(8,128)S(1)} %copy.491, f32[2,5,64,256]{3,2,1,0:T(8,128)S(1)} %copy.490, f32[2,5,64,256]{3,2,1,0:T(8,128)S(1)} %copy.489, f32[2,5,64,256]{3,2,1,0:T(8,128)} %copy.488), kind=kLoop, calls=%fused_computation.29 | loop fusion | flops 1179648 | bytes 4456448 | tf_op jit(solution)/shard_map/add | solution.py:61
  122.9 1.4 copy.445
  125.5 2.1 %slice.319 = f32[2,5,64,256]{3,2,1,0:T(8,128)} slice(f32[2,9,64,256]{3,2,1,0:T(8,128)} %pad_add_fusion), slice={[0:2], [2:7], [0:64], [0:256]} | slice | bytes 1310720 | tf_op jit(solution)/shard_map/slice | solution.py:210
  127.6 4.8 %collective-permute-start.9 = (f32[2,2,64,256]{3,2,1,0:T(8,128)}, f32[2,2,64,256]{3,2,1,0:T(8,128)S(1)}, u32[]{:S(2)}, u32[]{:S(2)}) collective-permute-start(f32[2,2,64,256]{3,2,1,0:T(8,128)} %get-tuple-element.61), channel_id=1, source_target_pairs={{8,0},{16,8},{24,16},{32,24},{40,32},{48,40},{56,48},{64,56},{72,6... | collective-permute-start | bytes 786440 | tf_op jit(solution)/shard_map/ppermute | solution.py:21
  132.4 4.8 %collective-permute-start.7 = (f32[2,2,64,256]{3,2,1,0:T(8,128)}, f32[2,2,64,256]{3,2,1,0:T(8,128)}, u32[]{:S(2)}, u32[]{:S(2)}) collective-permute-start(f32[2,2,64,256]{3,2,1,0:T(8,128)} %get-tuple-element.63), channel_id=1, source_target_pairs={{8,0},{16,8},{24,16},{32,24},{40,32},{48,40},{56,48},{64,56},{72,6... | collective-permute-start | bytes 786440 | tf_op jit(solution)/shard_map/ppermute | solution.py:21
  138.0 1.4 fusion.43
  139.5 1.9 %fusion.36 = f32[2,5,64,256]{3,2,1,0:T(8,128)} fusion(f32[2,5,64,256]{3,2,1,0:T(8,128)} %slice.319, f32[2,2,64,256]{3,2,1,0:T(8,128)} %collective-permute-done.8, f32[2,5,64,256]{3,2,1,0:T(8,128)S(1)} %copy.497, f32[2,5,64,256]{3,2,1,0:T(8,128)S(1)} %copy-done.3, f32[2,5,64,256]{3,2,1,0:T(8,128)S(1)} %copy-done.5, f32[2,5,64,256]{3,2,1,0:T(8,128)S(1)} %copy-done.7, ...), kind=kLoop, calls=%fused_computation.76 | loop fusion | flops 327680 | bytes 3801088 | tf_op jit(solution)/shard_map/scatter-add | solution.py:210
  141.4 3.1 %collective-permute-done.6 = f32[2,2,64,256]{3,2,1,0:T(8,128)} collective-permute-done((f32[2,2,64,256]{3,2,1,0:T(8,128)}, f32[2,2,64,256]{3,2,1,0:T(8,128)}, u32[]{:S(2)}, u32[]{:S(2)}) %collective-permute-start.6) | collective-permute-done | bytes 262176 | tf_op jit(solution)/shard_map/ppermute | solution.py:19
  (155 shorter events, 21.7 us)
Async XLA Ops:
  7.2 19.3 %copy-start.30 = (bf16[16,40,256]{2,1,0:T(8,128)(2,1)S(1)}, bf16[16,40,256]{2,1,0:T(8,128)(2,1)}, u32[]{:S(2)}) copy-start(bf16[16,40,256]{2,1,0:T(8,128)(2,1)} %param.15) | copy-start | bytes 983044
  7.2 130.0 %reduce-scatter.4.cloned.1.call-start = ((), (), s32[]{:S(2)}) async-start(), calls=%async_computation.1 | async-start | bytes 24576
  8.1 30.8 %collective-permute-start.2 = (s32[2,2,64]{2,0,1:T(2,128)S(1)}, s32[2,2,64]{2,0,1:T(2,128)S(1)}, u32[]{:S(2)}, u32[]{:S(2)}) collective-permute-start(s32[2,2,64]{2,0,1:T(2,128)S(1)} %get-tuple-element.97), channel_id=1, source_target_pairs={{0,8},{8,16},{16,24},{24,32},{32,40},{40,48},{48,56},{56,64},{64,7... | collective-permute-start | bytes 3080 | tf_op jit(solution)/shard_map/ppermute | solution.py:19
  10.3 28.7 %collective-permute-start.3 = (s32[2,2,64]{2,0,1:T(2,128)S(1)}, s32[2,2,64]{2,0,1:T(2,128)S(1)}, u32[]{:S(2)}, u32[]{:S(2)}) collective-permute-start(s32[2,2,64]{2,0,1:T(2,128)S(1)} %get-tuple-element.96), channel_id=1, source_target_pairs={{8,0},{16,8},{24,16},{32,24},{40,32},{48,40},{56,48},{64,56},{72,6... | collective-permute-start | bytes 3080 | tf_op jit(solution)/shard_map/ppermute | solution.py:21
  16.9 10.0 %copy-start.31 = (s32[2,5]{1,0:T(2,128)S(1)}, s32[2,5]{1,0:T(2,128)}, u32[]{:S(2)}) copy-start(s32[2,5]{1,0:T(2,128)} %param.21) | copy-start | bytes 124
  18.6 20.6 %collective-permute-start.1 = (bf16[2,2,64,256]{3,2,1,0:T(8,128)(2,1)}, bf16[2,2,64,256]{3,2,1,0:T(8,128)(2,1)}, u32[]{:S(2)}, u32[]{:S(2)}) collective-permute-start(bf16[2,2,64,256]{3,2,1,0:T(8,128)(2,1)} %get-tuple-element.83), channel_id=1, source_target_pairs={{8,0},{16,8},{24,16},{32,24},{40,32},{48,40},{56,48},{64,56},{72,6... | collective-permute-start | bytes 393224 | tf_op jit(solution)/shard_map/ppermute | solution.py:21
  20.0 19.2 %collective-permute-start = (bf16[2,2,64,256]{3,2,1,0:T(8,128)(2,1)}, bf16[2,2,64,256]{3,2,1,0:T(8,128)(2,1)}, u32[]{:S(2)}, u32[]{:S(2)}) collective-permute-start(bf16[2,2,64,256]{3,2,1,0:T(8,128)(2,1)} %get-tuple-element.84), channel_id=1, source_target_pairs={{0,8},{8,16},{16,24},{24,32},{32,40},{40,48},{48,56},{56,64},{64,7... | collective-permute-start | bytes 393224 | tf_op jit(solution)/shard_map/ppermute | solution.py:19
  21.8 10.2 %copy-start.32 = (s32[2,5]{1,0:T(2,128)S(1)}, s32[2,5]{1,0:T(2,128)}, u32[]{:S(2)}) copy-start(s32[2,5]{1,0:T(2,128)} %param.20) | copy-start | bytes 124
  21.8 31.0 %collective-permute-start.5 = (bf16[2,2,64,256]{3,2,1,0:T(8,128)(2,1)}, bf16[2,2,64,256]{3,2,1,0:T(8,128)(2,1)}, u32[]{:S(2)}, u32[]{:S(2)}) collective-permute-start(bf16[2,2,64,256]{3,2,1,0:T(8,128)(2,1)} %get-tuple-element.77), channel_id=1, source_target_pairs={{8,0},{16,8},{24,16},{32,24},{40,32},{48,40},{56,48},{64,56},{72,6... | collective-permute-start | bytes 393224 | tf_op jit(solution)/shard_map/ppermute | solution.py:21
  26.8 6.6 %copy-start.24 = (bf16[2,5,64,4,64]{4,3,2,1,0:T(4,128)(2,1)}, bf16[2,5,64,4,64]{4,3,2,1,0:T(4,128)(2,1)S(1)}, u32[]{:S(2)}) copy-start(bf16[2,5,64,4,64]{4,3,2,1,0:T(4,128)(2,1)S(1)} %reshape_reshape.14) | copy-start | bytes 983044
  32.0 30.3 %copy-start.20 = (f32[2,5,4,64,16]{3,4,1,0,2:T(8,128)}, f32[2,5,4,64,16]{3,4,1,0,2:T(8,128)S(1)}, u32[]{:S(2)}) copy-start(f32[2,5,4,64,16]{3,4,1,0,2:T(8,128)S(1)} %get-tuple-element.103) | copy-start | bytes 491524
  38.9 13.9 %collective-permute-start.4 = (bf16[2,2,64,256]{3,2,1,0:T(8,128)(2,1)S(1)}, bf16[2,2,64,256]{3,2,1,0:T(8,128)(2,1)}, u32[]{:S(2)}, u32[]{:S(2)}) collective-permute-start(bf16[2,2,64,256]{3,2,1,0:T(8,128)(2,1)S(1)} %get-tuple-element.78), channel_id=1, source_target_pairs={{0,8},{8,16},{16,24},{24,32},{32,40},{40,48},{48,56},{56,64},{64,7... | collective-permute-start | bytes 393224 | tf_op jit(solution)/shard_map/ppermute | solution.py:19
  50.8 1.9 %copy-start = (f32[2,5,4,320,64]{3,4,2,1,0:T(8,128)}, f32[2,5,4,320,64]{3,4,2,1,0:T(8,128)S(1)}, u32[]{:S(2)}) copy-start(f32[2,5,4,320,64]{3,4,2,1,0:T(8,128)S(1)} %get-tuple-element.101) | copy-start | bytes 9830404
  54.9 6.3 %copy-start.29 = (bf16[2,5,64,256]{3,2,1,0:T(8,128)(2,1)S(1)}, bf16[2,5,64,256]{3,2,1,0:T(8,128)(2,1)}, u32[]{:S(2)}) copy-start(bf16[2,5,64,256]{3,2,1,0:T(8,128)(2,1)} %get-tuple-element.67) | copy-start | bytes 983044
  63.7 5.3 %copy-start.27 = (bf16[2,5,64,4,64]{2,4,3,1,0:T(8,128)(2,1)S(1)}, bf16[2,5,64,4,64]{2,4,3,1,0:T(8,128)(2,1)}, u32[]{:S(2)}) copy-start(bf16[2,5,64,4,64]{2,4,3,1,0:T(8,128)(2,1)} %copy.436) | copy-start | bytes 983044
  69.0 4.6 %copy-start.1 = (f32[2,5,4,320,64]{3,4,2,1,0:T(8,128)S(1)}, f32[2,5,4,320,64]{3,4,2,1,0:T(8,128)}, u32[]{:S(2)}) copy-start(f32[2,5,4,320,64]{3,4,2,1,0:T(8,128)} %copy-done) | copy-start | bytes 9830404
  69.0 4.9 %copy-start.28 = (bf16[2,5,320,4,64]{2,4,3,1,0:T(8,128)(2,1)S(1)}, bf16[2,5,320,4,64]{2,4,3,1,0:T(8,128)(2,1)}, u32[]{:S(2)}) copy-start(bf16[2,5,320,4,64]{2,4,3,1,0:T(8,128)(2,1)} %concatenate.88) | copy-start | bytes 4915204
  93.4 3.1 %copy-start.2 = (f32[2,5,64,256]{3,2,1,0:T(8,128)S(1)}, f32[2,5,64,256]{3,2,1,0:T(8,128)}, u32[]{:S(2)}) copy-start(f32[2,5,64,256]{3,2,1,0:T(8,128)} %copy.496) | copy-start | bytes 1966084
  93.4 3.1 %copy-start.4 = (f32[2,5,64,256]{3,2,1,0:T(8,128)S(1)}, f32[2,5,64,256]{3,2,1,0:T(8,128)}, u32[]{:S(2)}) copy-start(f32[2,5,64,256]{3,2,1,0:T(8,128)} %copy.495) | copy-start | bytes 1966084
  93.5 3.1 %copy-start.6 = (f32[2,5,64,256]{3,2,1,0:T(8,128)S(1)}, f32[2,5,64,256]{3,2,1,0:T(8,128)}, u32[]{:S(2)}) copy-start(f32[2,5,64,256]{3,2,1,0:T(8,128)} %copy.494) | copy-start | bytes 1966084
  93.5 3.1 %copy-start.8 = (f32[2,5,64,256]{3,2,1,0:T(8,128)S(1)}, f32[2,5,64,256]{3,2,1,0:T(8,128)}, u32[]{:S(2)}) copy-start(f32[2,5,64,256]{3,2,1,0:T(8,128)} %copy.493) | copy-start | bytes 1966084
  96.6 1.0 copy-start.21
  97.6 1.3 copy-start.25
  97.8 1.6 %copy-start.22 = (bf16[2,5,4,64,320]{4,3,2,1,0:T(8,128)(2,1)S(1)}, bf16[2,5,4,64,320]{4,3,2,1,0:T(8,128)(2,1)}, u32[]{:S(2)}) copy-start(bf16[2,5,4,64,320]{4,3,2,1,0:T(8,128)(2,1)} %fusion) | copy-start | bytes 4915204
  97.8 1.7 %copy-start.23 = (bf16[2,5,64,4,64]{2,4,3,1,0:T(8,128)(2,1)S(1)}, bf16[2,5,64,4,64]{2,4,3,1,0:T(8,128)(2,1)}, u32[]{:S(2)}) copy-start(bf16[2,5,64,4,64]{2,4,3,1,0:T(8,128)(2,1)} %copy.447) | copy-start | bytes 983044
  112.5 9.5 %copy-start.10 = (f32[2,5,64,256]{3,2,1,0:T(8,128)}, f32[2,5,64,256]{3,2,1,0:T(8,128)S(1)}, u32[]{:S(2)}) copy-start(f32[2,5,64,256]{3,2,1,0:T(8,128)S(1)} %copy.492) | copy-start | bytes 1966084
  112.9 9.1 %copy-start.12 = (f32[2,5,64,256]{3,2,1,0:T(8,128)}, f32[2,5,64,256]{3,2,1,0:T(8,128)S(1)}, u32[]{:S(2)}) copy-start(f32[2,5,64,256]{3,2,1,0:T(8,128)S(1)} %copy.491) | copy-start | bytes 1966084
  114.8 7.2 %copy-start.14 = (f32[2,5,64,256]{3,2,1,0:T(8,128)}, f32[2,5,64,256]{3,2,1,0:T(8,128)S(1)}, u32[]{:S(2)}) copy-start(f32[2,5,64,256]{3,2,1,0:T(8,128)S(1)} %copy.490) | copy-start | bytes 1966084
  116.8 5.2 %copy-start.16 = (f32[2,5,64,256]{3,2,1,0:T(8,128)}, f32[2,5,64,256]{3,2,1,0:T(8,128)S(1)}, u32[]{:S(2)}) copy-start(f32[2,5,64,256]{3,2,1,0:T(8,128)S(1)} %copy.489) | copy-start | bytes 1966084
  119.6 2.4 %copy-start.18 = (f32[2,5,64,256]{3,2,1,0:T(8,128)S(1)}, f32[2,5,64,256]{3,2,1,0:T(8,128)}, u32[]{:S(2)}) copy-start(f32[2,5,64,256]{3,2,1,0:T(8,128)} %copy.488) | copy-start | bytes 1966084
  125.5 14.0 %copy-start.3 = (f32[2,5,64,256]{3,2,1,0:T(8,128)S(1)}, f32[2,5,64,256]{3,2,1,0:T(8,128)}, u32[]{:S(2)}) copy-start(f32[2,5,64,256]{3,2,1,0:T(8,128)} %copy.496) | copy-start | bytes 1966084
  125.5 14.0 %copy-start.5 = (f32[2,5,64,256]{3,2,1,0:T(8,128)S(1)}, f32[2,5,64,256]{3,2,1,0:T(8,128)}, u32[]{:S(2)}) copy-start(f32[2,5,64,256]{3,2,1,0:T(8,128)} %copy.495) | copy-start | bytes 1966084
  125.5 14.0 %copy-start.7 = (f32[2,5,64,256]{3,2,1,0:T(8,128)S(1)}, f32[2,5,64,256]{3,2,1,0:T(8,128)}, u32[]{:S(2)}) copy-start(f32[2,5,64,256]{3,2,1,0:T(8,128)} %copy.494) | copy-start | bytes 1966084
  125.5 14.0 %copy-start.9 = (f32[2,5,64,256]{3,2,1,0:T(8,128)S(1)}, f32[2,5,64,256]{3,2,1,0:T(8,128)}, u32[]{:S(2)}) copy-start(f32[2,5,64,256]{3,2,1,0:T(8,128)} %copy.493) | copy-start | bytes 1966084
  127.6 11.8 %collective-permute-start.8 = (f32[2,2,64,256]{3,2,1,0:T(8,128)}, f32[2,2,64,256]{3,2,1,0:T(8,128)}, u32[]{:S(2)}, u32[]{:S(2)}) collective-permute-start(f32[2,2,64,256]{3,2,1,0:T(8,128)} %get-tuple-element.62), channel_id=1, source_target_pairs={{0,8},{8,16},{16,24},{24,32},{32,40},{40,48},{48,56},{56,64},{64,7... | collective-permute-start | bytes 786440 | tf_op jit(solution)/shard_map/ppermute | solution.py:19
  127.6 17.9 %collective-permute-start.9 = (f32[2,2,64,256]{3,2,1,0:T(8,128)}, f32[2,2,64,256]{3,2,1,0:T(8,128)S(1)}, u32[]{:S(2)}, u32[]{:S(2)}) collective-permute-start(f32[2,2,64,256]{3,2,1,0:T(8,128)} %get-tuple-element.61), channel_id=1, source_target_pairs={{8,0},{16,8},{24,16},{32,24},{40,32},{48,40},{56,48},{64,56},{72,6... | collective-permute-start | bytes 786440 | tf_op jit(solution)/shard_map/ppermute | solution.py:21
  132.4 12.0 %collective-permute-start.6 = (f32[2,2,64,256]{3,2,1,0:T(8,128)}, f32[2,2,64,256]{3,2,1,0:T(8,128)}, u32[]{:S(2)}, u32[]{:S(2)}) collective-permute-start(f32[2,2,64,256]{3,2,1,0:T(8,128)} %get-tuple-element.64), channel_id=1, source_target_pairs={{0,8},{8,16},{16,24},{24,32},{32,40},{40,48},{48,56},{56,64},{64,7... | collective-permute-start | bytes 786440 | tf_op jit(solution)/shard_map/ppermute | solution.py:19
  132.4 13.2 %collective-permute-start.7 = (f32[2,2,64,256]{3,2,1,0:T(8,128)}, f32[2,2,64,256]{3,2,1,0:T(8,128)}, u32[]{:S(2)}, u32[]{:S(2)}) collective-permute-start(f32[2,2,64,256]{3,2,1,0:T(8,128)} %get-tuple-element.63), channel_id=1, source_target_pairs={{8,0},{16,8},{24,16},{32,24},{40,32},{48,40},{56,48},{64,56},{72,6... | collective-permute-start | bytes 786440 | tf_op jit(solution)/shard_map/ppermute | solution.py:21
  138.0 6.5 %slice-start = ((f32[2,9,64,256]{3,2,1,0:T(8,128)}), f32[2,5,64,256]{3,2,1,0:T(8,128)S(1)}, s32[]{:S(2)}) async-start(f32[2,9,64,256]{3,2,1,0:T(8,128)} %pad_add_fusion.1), calls=%async_computation.2 | async-start | bytes 1310720 | tf_op jit(solution)/shard_map/slice | solution.py:208
  139.4 5.1 %copy-start.11 = (f32[2,5,64,256]{3,2,1,0:T(8,128)S(1)}, f32[2,5,64,256]{3,2,1,0:T(8,128)}, u32[]{:S(2)}) copy-start(f32[2,5,64,256]{3,2,1,0:T(8,128)} %copy-done.10) | copy-start | bytes 1966084
  139.4 5.1 %copy-start.13 = (f32[2,5,64,256]{3,2,1,0:T(8,128)S(1)}, f32[2,5,64,256]{3,2,1,0:T(8,128)}, u32[]{:S(2)}) copy-start(f32[2,5,64,256]{3,2,1,0:T(8,128)} %copy-done.12) | copy-start | bytes 1966084
  139.4 5.1 %copy-start.15 = (f32[2,5,64,256]{3,2,1,0:T(8,128)S(1)}, f32[2,5,64,256]{3,2,1,0:T(8,128)}, u32[]{:S(2)}) copy-start(f32[2,5,64,256]{3,2,1,0:T(8,128)} %copy-done.14) | copy-start | bytes 1966084
  139.4 5.1 %copy-start.17 = (f32[2,5,64,256]{3,2,1,0:T(8,128)S(1)}, f32[2,5,64,256]{3,2,1,0:T(8,128)}, u32[]{:S(2)}) copy-start(f32[2,5,64,256]{3,2,1,0:T(8,128)} %copy-done.16) | copy-start | bytes 1966084
  139.4 5.1 %copy-start.19 = (f32[2,5,64,256]{3,2,1,0:T(8,128)S(1)}, f32[2,5,64,256]{3,2,1,0:T(8,128)}, u32[]{:S(2)}) copy-start(f32[2,5,64,256]{3,2,1,0:T(8,128)} %copy.488) | copy-start | bytes 1966084
  141.4 4.2 %copy-start.26 = (f32[2,5,64,256]{3,2,1,0:T(8,128)S(1)}, f32[2,5,64,256]{3,2,1,0:T(8,128)}, u32[]{:S(2)}) copy-start(f32[2,5,64,256]{3,2,1,0:T(8,128)} %fusion.36) | copy-start | bytes 1966084
Sparse Core Ops, SparseCore 0:
  104.7 11.7 reduce-scatter.3
where the time goes:
time: 156 us; the launch traced here: 155 us
  local copies, waits for them, and re-layouts  72 us (46%)
  starting transfers between devices  24.5 us (16%)
  matrix products  20 us (13%)
  other arithmetic  17.2 us (11%)
  between operations  14.7 us (9%)
  blocking collectives  3.59 us (2%)
  waiting for transfers between devices  3.11 us (2%)
    unnamed x78, local copies, waits for them, and re-layouts  22.7 us
    ppermute x5, starting transfers between devices, extended_2(): lax.ppermute(head, axis, [((i + 1) % count, i) for i in range(count)])  22.3 us
    concatenate x7, local copies, waits for them, and re-layouts, window_blocks(): jnp.concatenate([extended[:, step:step + lon_blocks] for step in range(5)...  12.5 us
    slice x10, local copies, waits for them, and re-layouts, window_blocks(): extended[:, step:step + lon_blocks]  11.8 us
    slice x2, local copies, waits for them, and re-layouts, fold_blocks(): piece = grads[:, :, step * cells:(step + 1) * cells]  9.79 us
    add x2, other arithmetic, fold_blocks(): folded = piece if folded is None else folded + piece  5.51 us
    dot_general x1, matrix products, local(): jnp.einsum('abhqk,abkhd->abqhd', window_lower_bound, candidate_values, pr...  4.53 us
    all_gather x1, blocking collectives, local(): gathered = lax.all_gather(pooled, 'lat', axis=0, tiled=True)  3.59 us
  transfers between devices with their start and end apart: 11, of which 1 were waited for; matrix products, arithmetic and copies ran while one was open for 34% of the time, Pallas kernels for 0%

commit v1 on v0

--- a/solution.py
+++ b/solution.py
@@ -91,7 +91,12 @@
         weights_low, value_blocks.reshape(cell_count, features), preferred_element_type=jnp.float32
     )
     pooled = (jnp.stack([pooled_k, pooled_v], axis=1) / divisor[:, None, None]).astype(jnp.bfloat16)
-    gathered = lax.all_gather(pooled, "lat", axis=0, tiled=True)
+    gathered = jnp.concatenate(
+        lax.all_to_all(
+            jnp.stack(lax.axis_size("lat") * [pooled]), concat_axis=0, axis_name="lat", split_axis=0
+        ),
+        0,
+    )
     reg_count = gathered.shape[0]
     register_key_rows = gathered[:, 0].reshape(reg_count, head_count, HS)
     register_value_rows = gathered[:, 1].reshape(reg_count, head_count, HS)

time: 156 us -> 158 us (1.013)
  starting transfers between devices: 24.5 us -> 28.4 us
  blocking collectives: 3.59 us -> 0 us
    all_to_all x0 -> x1, starting transfers between devices: none -> 6.47 us  [local(): lax.all_to_all(jnp.stack(lax.axis_size('lat') * [pooled]), concat_axis=0,...]
    all_gather x1 -> x0, blocking collectives: 3.59 us -> none  [local(): gathered = lax.all_gather(pooled, 'lat', axis=0, tiled=True)]
    ppermute x5, starting transfers between devices: 2.22 us -> 0.18 us  [extended_2(): lax.ppermute(tail, axis, [(i, (i + 1) % count) for i in range(count)])]
  transfers between devices with their start and end apart: 11 -> 12, of which waited for: 1 -> 1; matrix products, arithmetic and copies ran while one was open for 34% -> 32% of each run, Pallas kernels for 0% -> 0%
where the time goes in v1:
time: 158 us; the launch traced here: 156 us
  local copies, waits for them, and re-layouts  72.7 us (46%)
  starting transfers between devices  28.4 us (18%)
  matrix products  20 us (13%)
  other arithmetic  17.9 us (11%)
  between operations  14.8 us (9%)
  waiting for transfers between devices  2.15 us (1%)
    unnamed x78, local copies, waits for them, and re-layouts  22.8 us
    ppermute x5, starting transfers between devices, extended_2(): lax.ppermute(head, axis, [((i + 1) % count, i) for i in range(count)])  21.7 us
    concatenate x7, local copies, waits for them, and re-layouts, window_blocks(): jnp.concatenate([extended[:, step:step + lon_blocks] for step in range(5)...  12.4 us
    slice x10, local copies, waits for them, and re-layouts, window_blocks(): extended[:, step:step + lon_blocks]  11.8 us
    slice x2, local copies, waits for them, and re-layouts, fold_blocks(): piece = grads[:, :, step * cells:(step + 1) * cells]  9.75 us
    all_to_all x1, starting transfers between devices, local(): lax.all_to_all(jnp.stack(lax.axis_size('lat') * [pooled]), concat_axis=0,...  6.47 us
    add x2, other arithmetic, fold_blocks(): folded = piece if folded is None else folded + piece  5.49 us
    dot_general x1, matrix products, local(): jnp.einsum('abhqk,abkhd->abqhd', window_lower_bound, candidate_values, pr...  4.53 us
  transfers between devices with their start and end apart: 12, of which 1 were waited for; matrix products, arithmetic and copies ran while one was open for 32% of the time, Pallas kernels for 0%

profile of v1, /device:TPU:1, one launch (start us, length us, event | category | flops | bytes accessed | tf_op | source)
XLA Modules:
  0.0 155.9 jit_solution(14045355742687686868)
XLA Ops:
  12.1 6.5 %all-to-all-start = ((bf16[2,8,2,256]{3,1,2,0:T(8,128)(2,1)}), bf16[2,8,2,256]{3,1,2,0:T(8,128)(2,1)S(1)}, u32[]{:S(2)}, u32[]{:S(2)}) async-start(bf16[2,8,2,256]{3,1,2,0:T(8,128)(2,1)} %pad_maximum_fusion.4), calls=%async_computation | async-start | bytes 32768 | tf_op jit(solution)/shard_map/all_to_all | solution.py:95
  18.8 6.1 %collective-permute-start.3 = (s32[2,2,64]{2,0,1:T(2,128)S(1)}, s32[2,2,64]{2,0,1:T(2,128)S(1)}, u32[]{:S(2)}, u32[]{:S(2)}) collective-permute-start(s32[2,2,64]{2,0,1:T(2,128)S(1)} %get-tuple-element.96), channel_id=1, source_target_pairs={{8,0},{16,8},{24,16},{32,24},{40,32},{48,40},{56,48},{64,56},{72,6... | collective-permute-start | bytes 3080 | tf_op jit(solution)/shard_map/ppermute | solution.py:21
  25.6 1.4 collective-permute-start.1
  27.7 4.7 %collective-permute-start.5 = (bf16[2,2,64,256]{3,2,1,0:T(8,128)(2,1)}, bf16[2,2,64,256]{3,2,1,0:T(8,128)(2,1)}, u32[]{:S(2)}, u32[]{:S(2)}) collective-permute-start(bf16[2,2,64,256]{3,2,1,0:T(8,128)(2,1)} %get-tuple-element.77), channel_id=1, source_target_pairs={{8,0},{16,8},{24,16},{32,24},{40,32},{48,40},{56,48},{64,56},{72,6... | collective-permute-start | bytes 393224 | tf_op jit(solution)/shard_map/ppermute | solution.py:21
  33.6 1.1 copy.387
  37.0 1.2 copy.349
  38.2 1.1 copy.373
  39.3 1.1 copy.376
  40.8 1.1 pad_maximum_fusion.2
  41.9 1.1 copy.344
  43.0 1.1 copy.345
  44.1 1.1 copy.347
  45.2 1.1 copy.348
  46.3 4.1 %concatenate.84 = bf16[2,5,320,4,64]{2,4,3,1,0:T(8,128)(2,1)S(1)} concatenate(bf16[2,5,64,4,64]{2,4,3,1,0:T(8,128)(2,1)} %bitcast.192, bf16[2,5,64,4,64]{2,4,3,1,0:T(8,128)(2,1)} %bitcast.194, bf16[2,5,64,4,64]{2,4,3,1,0:T(8,128)(2,1)} %copy.349, bf16[2,5,64,4,64]{2,4,3,1,0:T(8,128)(2,1)} %bitcast.196, bf16[2,5,64,4,64]{2,4,3,1,0:T(8,128)(2,1)} %bitcast.198), dimensions={2} | concatenate | bytes 3276800 | tf_op jit(solution)/shard_map/concatenate | solution.py:52
  50.4 1.9 %bitcast_reduce_fusion = (f32[2,5,4,64]{3,2,1,0:T(4,128)S(1)}, f32[2,5,4,320,64]{3,4,2,1,0:T(8,128)S(1)}) fusion(pred[2,5,320]{2,1,0:T(8,128)(4,1)S(1)} %copy.355, bf16[2,5,64,4,64]{2,4,3,1,0:T(8,128)(2,1)} %copy.387, bf16[2,5,320,4,64]{2,4,3,1,0:T(8,128)(2,1)S(1)} %concatenate.84), kind=kOutput, calls=%fused_computation.4 | convolution fusion | flops 107312640 | bytes 5256320 | tf_op jit(solution)/shard_map/abqhd,abkhd->abhqk/dot_general | solution.py:127
  52.4 1.3 fusion.3
  54.4 2.1 %pad_maximum_fusion = (bf16[2,5,64,256]{3,2,1,0:T(8,128)(2,1)}, bf16[2,5,64,256]{3,2,1,0:T(8,128)(2,1)}, bf16[2,5,64,256]{3,2,1,0:T(8,128)(2,1)}, bf16[2,5,64,256]{3,2,1,0:T(8,128)(2,1)}) fusion(bf16[2,2,64,256]{3,2,1,0:T(8,128)(2,1)} %collective-permute-done.5, bf16[2,5,64,256]{3,2,1,0:T(8,128)(2,1)S(1)} %bitcast.187, ...), kind=kLoop, calls=%fused_computation.62 | loop fusion | flops 655360 | bytes 1900544 | tf_op jit(solution)/shard_map/concatenate | solution.py:17
  56.5 2.2 %copy.368 = bf16[2,5,64,256]{2,3,1,0:T(8,128)(2,1)} copy(bf16[2,5,64,256]{3,2,1,0:T(8,128)(2,1)} %get-tuple-element.75) | data formatting | bytes 655360 | tf_op jit(solution)/shard_map/slice | solution.py:52
  58.6 2.1 %copy.369 = bf16[2,5,64,256]{2,3,1,0:T(8,128)(2,1)} copy(bf16[2,5,64,256]{3,2,1,0:T(8,128)(2,1)} %get-tuple-element.76) | data formatting | bytes 655360 | tf_op jit(solution)/shard_map/slice | solution.py:52
  60.7 2.1 %copy.371 = bf16[2,5,64,256]{2,3,1,0:T(8,128)(2,1)} copy(bf16[2,5,64,256]{3,2,1,0:T(8,128)(2,1)} %get-tuple-element.68) | data formatting | bytes 655360 | tf_op jit(solution)/shard_map/slice | solution.py:52
  62.8 1.1 copy.372
  63.9 1.4 convolution_bitcast_fusion.3
  65.4 5.3 %concatenate.95 = bf16[2,5,320,4,64]{2,4,3,1,0:T(8,128)(2,1)} concatenate(bf16[2,5,64,4,64]{2,4,3,1,0:T(8,128)(2,1)} %bitcast.191, bf16[2,5,64,4,64]{2,4,3,1,0:T(8,128)(2,1)} %bitcast.193, bf16[2,5,64,4,64]{2,4,3,1,0:T(8,128)(2,1)} %copy.373, bf16[2,5,64,4,64]{2,4,3,1,0:T(8,128)(2,1)} %bitcast.195, bf16[2,5,64,4,64]{2,4,3,1,0:T(8,128)(2,1)} %bitcast.197), dimensions={2} | concatenate | bytes 3276800 | tf_op jit(solution)/shard_map/concatenate | solution.py:52
  70.6 4.5 %fusion.12 = f32[2,5,64,4]{2,3,1,0:T(4,128)S(1)} fusion(f32[2,5,64,4,64]{2,4,3,1,0:T(8,128)} %convolution_bitcast_fusion.3, bf16[2,5,320,4,64]{2,4,3,1,0:T(8,128)(2,1)} %concatenate.95, bf16[2,5,64,4,64]{2,4,3,1,0:T(8,128)(2,1)S(1)} %copy-done.27, f32[2,5,4,320,64]{3,4,2,1,0:T(8,128)} %copy-done, f32[2,5,4,64]{3,2,1,0:T(4,128)S(1)} %fusion.47, ...), kind=kOutput, calls=%fused_computation.22 | convolution fusion | flops 109606400 | bytes 5921920 | tf_op jit(solution)/shard_map/abhqk,abkhd->abqhd/dot_general | solution.py:145
  75.5 2.7 %fusion = bf16[2,5,4,64,320]{4,3,2,1,0:T(8,128)(2,1)} fusion(f32[2,5,4,320,64]{3,4,2,1,0:T(8,128)S(1)} %copy-done.1, bf16[2,5,64,4,64]{2,4,3,1,0:T(8,128)(2,1)S(1)} %copy-done.27, bf16[2,5,320,4,64]{2,4,3,1,0:T(8,128)(2,1)S(1)} %copy-done.28, f32[2,5,4,64]{3,2,1,0:T(4,128)S(1)} %bitcast.218, f32[2,5,4,64]{3,2,1,0:T(4,128)S(1)} %fusion.47, ...), kind=kOutput, calls=%fused_computation.1 | convolution fusion | flops 110592000 | bytes 6904960 | tf_op jit(solution)/shard_map/abqhd,abkhd->abhqk/dot_general | solution.py:159
  78.2 1.4 fusion.65
  79.5 3.6 %fusion.68 = (f32[2,5,64,256]{2,3,1,0:T(8,128)}, f32[2,5,64,256]{2,3,1,0:T(8,128)}, f32[2,5,64,256]{2,3,1,0:T(8,128)}, f32[2,5,64,256]{2,3,1,0:T(8,128)}, f32[2,5,64,256]{2,3,1,0:T(8,128)}) fusion(f32[2,5,320,256]{2,3,1,0:T(8,128)S(1)} %bitcast.184), kind=kLoop, calls=%fused_computation.134 | loop fusion | bytes 6553600 | tf_op jit(solution)/shard_map/slice | solution.py:59
  83.2 1.7 %copy.437 = f32[2,5,64,256]{3,2,1,0:T(8,128)S(1)} copy(f32[2,5,64,256]{2,3,1,0:T(8,128)} %get-tuple-element.55) | data formatting | bytes 1310720
  84.9 2.5 %copy.436 = f32[2,5,64,256]{3,2,1,0:T(8,128)} copy(f32[2,5,64,256]{2,3,1,0:T(8,128)} %get-tuple-element.52) | data formatting | bytes 1310720
  87.4 2.6 %copy.435 = f32[2,5,64,256]{3,2,1,0:T(8,128)} copy(f32[2,5,64,256]{2,3,1,0:T(8,128)} %get-tuple-element.53) | data formatting | bytes 1310720
  90.0 2.6 %copy.434 = f32[2,5,64,256]{3,2,1,0:T(8,128)} copy(f32[2,5,64,256]{2,3,1,0:T(8,128)} %get-tuple-element.54) | data formatting | bytes 1310720
  92.6 2.6 %copy.433 = f32[2,5,64,256]{3,2,1,0:T(8,128)} copy(f32[2,5,64,256]{2,3,1,0:T(8,128)} %get-tuple-element.51) | data formatting | bytes 1310720
  95.1 3.1 %pad_add_fusion = f32[2,9,64,256]{3,2,1,0:T(8,128)} fusion(f32[2,5,64,256]{3,2,1,0:T(8,128)S(1)} %copy.437, f32[2,5,64,256]{3,2,1,0:T(8,128)} %copy.436, f32[2,5,64,256]{3,2,1,0:T(8,128)} %copy.435, f32[2,5,64,256]{3,2,1,0:T(8,128)} %copy.434, f32[2,5,64,256]{3,2,1,0:T(8,128)} %copy.433), kind=kLoop, calls=%fused_computation.28 | loop fusion | flops 1179648 | bytes 4456448 | tf_op jit(solution)/shard_map/add | solution.py:61
  101.2 2.6 %convolution_multiply_fusion = f32[2,5,4,320,64]{3,4,2,1,0:T(8,128)} fusion(bf16[2,5,64,4,64]{2,4,3,1,0:T(8,128)(2,1)S(1)} %copy-done.23, bf16[2,5,4,64,320]{4,3,2,1,0:T(8,128)(2,1)S(1)} %copy-done.22), kind=kOutput, calls=%fused_computation.12 | convolution fusion | flops 105676800 | bytes 5242880 | tf_op jit(solution)/shard_map/abhqk,abqhd->abkhd/dot_general | solution.py:199
  103.8 1.7 %fusion.11 = bf16[2,5,64,4,64]{2,4,3,1,0:T(8,128)(2,1)} fusion(f32[2,5,64,4,64]{2,4,3,1,0:T(8,128)S(1)} %convolution_bitcast_fusion.2, bf16[2,5,320,4,64]{2,4,3,1,0:T(8,128)(2,1)S(1)} %concatenate.84, bf16[2,5,4,64,320]{4,3,2,1,0:T(8,128)(2,1)S(1)} %copy-done.22), kind=kOutput, calls=%fused_computation.21 | convolution fusion | flops 105349120 | bytes 4259840 | tf_op jit(solution)/shard_map/abhqk,abkhd->abqhd/dot_general | solution.py:170
  106.3 6.2 %fusion.69 = (f32[2,5,64,256]{2,3,1,0:T(8,128)}, f32[2,5,64,256]{2,3,1,0:T(8,128)S(1)}, f32[2,5,64,256]{2,3,1,0:T(8,128)}, f32[2,5,64,256]{2,3,1,0:T(8,128)}, f32[2,5,64,256]{2,3,1,0:T(8,128)}) fusion(f32[2,5,320,256]{2,3,1,0:T(8,128)} %bitcast.183), kind=kLoop, calls=%fused_computation.135 | loop fusion | bytes 6553600 | tf_op jit(solution)/shard_map/slice | solution.py:59
  112.5 1.7 %copy.432 = f32[2,5,64,256]{3,2,1,0:T(8,128)S(1)} copy(f32[2,5,64,256]{2,3,1,0:T(8,128)} %get-tuple-element.60) | data formatting | bytes 1310720
  114.6 1.9 %copy.430 = f32[2,5,64,256]{3,2,1,0:T(8,128)S(1)} copy(f32[2,5,64,256]{2,3,1,0:T(8,128)} %get-tuple-element.58) | data formatting | bytes 1310720
  116.5 1.9 %copy.429 = f32[2,5,64,256]{3,2,1,0:T(8,128)S(1)} copy(f32[2,5,64,256]{2,3,1,0:T(8,128)} %get-tuple-element.59) | data formatting | bytes 1310720
  118.5 2.8 %copy.428 = f32[2,5,64,256]{3,2,1,0:T(8,128)} copy(f32[2,5,64,256]{2,3,1,0:T(8,128)} %get-tuple-element.56) | data formatting | bytes 1310720
  121.3 2.4 %pad_add_fusion.1 = f32[2,9,64,256]{3,2,1,0:T(8,128)} fusion(f32[2,5,64,256]{3,2,1,0:T(8,128)S(1)} %copy.432, f32[2,5,64,256]{3,2,1,0:T(8,128)S(1)} %copy.431, f32[2,5,64,256]{3,2,1,0:T(8,128)S(1)} %copy.430, f32[2,5,64,256]{3,2,1,0:T(8,128)S(1)} %copy.429, f32[2,5,64,256]{3,2,1,0:T(8,128)} %copy.428), kind=kLoop, calls=%fused_computation.29 | loop fusion | flops 1179648 | bytes 4456448 | tf_op jit(solution)/shard_map/add | solution.py:61
  124.6 1.4 copy.385
  127.2 2.1 %slice.319 = f32[2,5,64,256]{3,2,1,0:T(8,128)} slice(f32[2,9,64,256]{3,2,1,0:T(8,128)} %pad_add_fusion), slice={[0:2], [2:7], [0:64], [0:256]} | slice | bytes 1310720 | tf_op jit(solution)/shard_map/slice | solution.py:215
  129.3 4.8 %collective-permute-start.9 = (f32[2,2,64,256]{3,2,1,0:T(8,128)}, f32[2,2,64,256]{3,2,1,0:T(8,128)S(1)}, u32[]{:S(2)}, u32[]{:S(2)}) collective-permute-start(f32[2,2,64,256]{3,2,1,0:T(8,128)} %get-tuple-element.61), channel_id=1, source_target_pairs={{8,0},{16,8},{24,16},{32,24},{40,32},{48,40},{56,48},{64,56},{72,6... | collective-permute-start | bytes 786440 | tf_op jit(solution)/shard_map/ppermute | solution.py:21
  134.1 4.8 %collective-permute-start.7 = (f32[2,2,64,256]{3,2,1,0:T(8,128)}, f32[2,2,64,256]{3,2,1,0:T(8,128)}, u32[]{:S(2)}, u32[]{:S(2)}) collective-permute-start(f32[2,2,64,256]{3,2,1,0:T(8,128)} %get-tuple-element.63), channel_id=1, source_target_pairs={{8,0},{16,8},{24,16},{32,24},{40,32},{48,40},{56,48},{64,56},{72,6... | collective-permute-start | bytes 786440 | tf_op jit(solution)/shard_map/ppermute | solution.py:21
  139.7 1.4 fusion.43
  141.2 1.9 %fusion.36 = f32[2,5,64,256]{3,2,1,0:T(8,128)} fusion(f32[2,5,64,256]{3,2,1,0:T(8,128)} %slice.319, f32[2,2,64,256]{3,2,1,0:T(8,128)} %collective-permute-done.8, f32[2,5,64,256]{3,2,1,0:T(8,128)S(1)} %copy.437, f32[2,5,64,256]{3,2,1,0:T(8,128)S(1)} %copy-done.3, f32[2,5,64,256]{3,2,1,0:T(8,128)S(1)} %copy-done.5, f32[2,5,64,256]{3,2,1,0:T(8,128)S(1)} %copy-done.7, ...), kind=kLoop, calls=%fused_computation.76 | loop fusion | flops 327680 | bytes 3801088 | tf_op jit(solution)/shard_map/scatter-add | solution.py:215
  143.1 2.1 %collective-permute-done.6 = f32[2,2,64,256]{3,2,1,0:T(8,128)} collective-permute-done((f32[2,2,64,256]{3,2,1,0:T(8,128)}, f32[2,2,64,256]{3,2,1,0:T(8,128)}, u32[]{:S(2)}, u32[]{:S(2)}) %collective-permute-start.6) | collective-permute-done | bytes 262176 | tf_op jit(solution)/shard_map/ppermute | solution.py:19
  (158 shorter events, 22.0 us)
Async XLA Ops:
  7.2 25.3 %copy-start.30 = (bf16[16,40,256]{2,1,0:T(8,128)(2,1)S(1)}, bf16[16,40,256]{2,1,0:T(8,128)(2,1)}, u32[]{:S(2)}) copy-start(bf16[16,40,256]{2,1,0:T(8,128)(2,1)} %param.15) | copy-start | bytes 983044
  12.1 20.7 %all-to-all-start = ((bf16[2,8,2,256]{3,1,2,0:T(8,128)(2,1)}), bf16[2,8,2,256]{3,1,2,0:T(8,128)(2,1)S(1)}, u32[]{:S(2)}, u32[]{:S(2)}) async-start(bf16[2,8,2,256]{3,1,2,0:T(8,128)(2,1)} %pad_maximum_fusion.4), calls=%async_computation | async-start | bytes 32768 | tf_op jit(solution)/shard_map/all_to_all | solution.py:95
  18.5 120.3 %reduce-scatter.4.cloned.1.call-start = ((), (), s32[]{:S(2)}) async-start(), calls=%async_computation.2 | async-start | bytes 24576
  18.6 15.0 %copy-start.32 = (s32[2,5]{1,0:T(2,128)S(1)}, s32[2,5]{1,0:T(2,128)}, u32[]{:S(2)}) copy-start(s32[2,5]{1,0:T(2,128)} %param.20) | copy-start | bytes 124
  18.7 21.8 %collective-permute-start.2 = (s32[2,2,64]{2,0,1:T(2,128)S(1)}, s32[2,2,64]{2,0,1:T(2,128)S(1)}, u32[]{:S(2)}, u32[]{:S(2)}) collective-permute-start(s32[2,2,64]{2,0,1:T(2,128)S(1)} %get-tuple-element.97), channel_id=1, source_target_pairs={{0,8},{8,16},{16,24},{24,32},{32,40},{40,48},{48,56},{56,64},{64,7... | collective-permute-start | bytes 3080 | tf_op jit(solution)/shard_map/ppermute | solution.py:19
  18.8 21.7 %collective-permute-start.3 = (s32[2,2,64]{2,0,1:T(2,128)S(1)}, s32[2,2,64]{2,0,1:T(2,128)S(1)}, u32[]{:S(2)}, u32[]{:S(2)}) collective-permute-start(s32[2,2,64]{2,0,1:T(2,128)S(1)} %get-tuple-element.96), channel_id=1, source_target_pairs={{8,0},{16,8},{24,16},{32,24},{40,32},{48,40},{56,48},{64,56},{72,6... | collective-permute-start | bytes 3080 | tf_op jit(solution)/shard_map/ppermute | solution.py:21
  25.6 15.2 %collective-permute-start.1 = (bf16[2,2,64,256]{3,2,1,0:T(8,128)(2,1)}, bf16[2,2,64,256]{3,2,1,0:T(8,128)(2,1)}, u32[]{:S(2)}, u32[]{:S(2)}) collective-permute-start(bf16[2,2,64,256]{3,2,1,0:T(8,128)(2,1)} %get-tuple-element.83), channel_id=1, source_target_pairs={{8,0},{16,8},{24,16},{32,24},{40,32},{48,40},{56,48},{64,56},{72,6... | collective-permute-start | bytes 393224 | tf_op jit(solution)/shard_map/ppermute | solution.py:21
  27.0 13.8 %collective-permute-start = (bf16[2,2,64,256]{3,2,1,0:T(8,128)(2,1)}, bf16[2,2,64,256]{3,2,1,0:T(8,128)(2,1)}, u32[]{:S(2)}, u32[]{:S(2)}) collective-permute-start(bf16[2,2,64,256]{3,2,1,0:T(8,128)(2,1)} %get-tuple-element.84), channel_id=1, source_target_pairs={{0,8},{8,16},{16,24},{24,32},{32,40},{40,48},{48,56},{56,64},{64,7... | collective-permute-start | bytes 393224 | tf_op jit(solution)/shard_map/ppermute | solution.py:19
  27.7 26.6 %collective-permute-start.5 = (bf16[2,2,64,256]{3,2,1,0:T(8,128)(2,1)}, bf16[2,2,64,256]{3,2,1,0:T(8,128)(2,1)}, u32[]{:S(2)}, u32[]{:S(2)}) collective-permute-start(bf16[2,2,64,256]{3,2,1,0:T(8,128)(2,1)} %get-tuple-element.77), channel_id=1, source_target_pairs={{8,0},{16,8},{24,16},{32,24},{40,32},{48,40},{56,48},{64,56},{72,6... | collective-permute-start | bytes 393224 | tf_op jit(solution)/shard_map/ppermute | solution.py:21
  32.8 2.6 %copy-start.24 = (bf16[2,5,64,4,64]{4,3,2,1,0:T(4,128)(2,1)}, bf16[2,5,64,4,64]{4,3,2,1,0:T(4,128)(2,1)S(1)}, u32[]{:S(2)}) copy-start(bf16[2,5,64,4,64]{4,3,2,1,0:T(4,128)(2,1)S(1)} %reshape_reshape.14) | copy-start | bytes 983044
  33.6 30.3 %copy-start.20 = (f32[2,5,4,64,16]{3,4,1,0,2:T(8,128)}, f32[2,5,4,64,16]{3,4,1,0,2:T(8,128)S(1)}, u32[]{:S(2)}) copy-start(f32[2,5,4,64,16]{3,4,1,0,2:T(8,128)S(1)} %get-tuple-element.103) | copy-start | bytes 491524
  40.5 13.9 %collective-permute-start.4 = (bf16[2,2,64,256]{3,2,1,0:T(8,128)(2,1)S(1)}, bf16[2,2,64,256]{3,2,1,0:T(8,128)(2,1)}, u32[]{:S(2)}, u32[]{:S(2)}) collective-permute-start(bf16[2,2,64,256]{3,2,1,0:T(8,128)(2,1)S(1)} %get-tuple-element.78), channel_id=1, source_target_pairs={{0,8},{8,16},{16,24},{24,32},{32,40},{40,48},{48,56},{56,64},{64,7... | collective-permute-start | bytes 393224 | tf_op jit(solution)/shard_map/ppermute | solution.py:19
  52.3 1.9 %copy-start = (f32[2,5,4,320,64]{3,4,2,1,0:T(8,128)}, f32[2,5,4,320,64]{3,4,2,1,0:T(8,128)S(1)}, u32[]{:S(2)}) copy-start(f32[2,5,4,320,64]{3,4,2,1,0:T(8,128)S(1)} %get-tuple-element.101) | copy-start | bytes 9830404
  56.5 6.3 %copy-start.29 = (bf16[2,5,64,256]{3,2,1,0:T(8,128)(2,1)S(1)}, bf16[2,5,64,256]{3,2,1,0:T(8,128)(2,1)}, u32[]{:S(2)}) copy-start(bf16[2,5,64,256]{3,2,1,0:T(8,128)(2,1)} %get-tuple-element.67) | copy-start | bytes 983044
  65.4 5.3 %copy-start.27 = (bf16[2,5,64,4,64]{2,4,3,1,0:T(8,128)(2,1)S(1)}, bf16[2,5,64,4,64]{2,4,3,1,0:T(8,128)(2,1)}, u32[]{:S(2)}) copy-start(bf16[2,5,64,4,64]{2,4,3,1,0:T(8,128)(2,1)} %copy.376) | copy-start | bytes 983044
  70.6 4.6 %copy-start.1 = (f32[2,5,4,320,64]{3,4,2,1,0:T(8,128)S(1)}, f32[2,5,4,320,64]{3,4,2,1,0:T(8,128)}, u32[]{:S(2)}) copy-start(f32[2,5,4,320,64]{3,4,2,1,0:T(8,128)} %copy-done) | copy-start | bytes 9830404
  70.6 4.9 %copy-start.28 = (bf16[2,5,320,4,64]{2,4,3,1,0:T(8,128)(2,1)S(1)}, bf16[2,5,320,4,64]{2,4,3,1,0:T(8,128)(2,1)}, u32[]{:S(2)}) copy-start(bf16[2,5,320,4,64]{2,4,3,1,0:T(8,128)(2,1)} %concatenate.95) | copy-start | bytes 4915204
  95.1 3.1 %copy-start.2 = (f32[2,5,64,256]{3,2,1,0:T(8,128)S(1)}, f32[2,5,64,256]{3,2,1,0:T(8,128)}, u32[]{:S(2)}) copy-start(f32[2,5,64,256]{3,2,1,0:T(8,128)} %copy.436) | copy-start | bytes 1966084
  95.1 3.1 %copy-start.4 = (f32[2,5,64,256]{3,2,1,0:T(8,128)S(1)}, f32[2,5,64,256]{3,2,1,0:T(8,128)}, u32[]{:S(2)}) copy-start(f32[2,5,64,256]{3,2,1,0:T(8,128)} %copy.435) | copy-start | bytes 1966084
  95.1 3.1 %copy-start.6 = (f32[2,5,64,256]{3,2,1,0:T(8,128)S(1)}, f32[2,5,64,256]{3,2,1,0:T(8,128)}, u32[]{:S(2)}) copy-start(f32[2,5,64,256]{3,2,1,0:T(8,128)} %copy.434) | copy-start | bytes 1966084
  95.1 3.1 %copy-start.8 = (f32[2,5,64,256]{3,2,1,0:T(8,128)S(1)}, f32[2,5,64,256]{3,2,1,0:T(8,128)}, u32[]{:S(2)}) copy-start(f32[2,5,64,256]{3,2,1,0:T(8,128)} %copy.433) | copy-start | bytes 1966084
  98.2 1.0 copy-start.21
  99.2 1.3 copy-start.25
  99.5 1.6 %copy-start.22 = (bf16[2,5,4,64,320]{4,3,2,1,0:T(8,128)(2,1)S(1)}, bf16[2,5,4,64,320]{4,3,2,1,0:T(8,128)(2,1)}, u32[]{:S(2)}) copy-start(bf16[2,5,4,64,320]{4,3,2,1,0:T(8,128)(2,1)} %fusion) | copy-start | bytes 4915204
  99.5 1.7 %copy-start.23 = (bf16[2,5,64,4,64]{2,4,3,1,0:T(8,128)(2,1)S(1)}, bf16[2,5,64,4,64]{2,4,3,1,0:T(8,128)(2,1)}, u32[]{:S(2)}) copy-start(bf16[2,5,64,4,64]{2,4,3,1,0:T(8,128)(2,1)} %copy.387) | copy-start | bytes 983044
  114.2 9.5 %copy-start.10 = (f32[2,5,64,256]{3,2,1,0:T(8,128)}, f32[2,5,64,256]{3,2,1,0:T(8,128)S(1)}, u32[]{:S(2)}) copy-start(f32[2,5,64,256]{3,2,1,0:T(8,128)S(1)} %copy.432) | copy-start | bytes 1966084
  114.6 9.1 %copy-start.12 = (f32[2,5,64,256]{3,2,1,0:T(8,128)}, f32[2,5,64,256]{3,2,1,0:T(8,128)S(1)}, u32[]{:S(2)}) copy-start(f32[2,5,64,256]{3,2,1,0:T(8,128)S(1)} %copy.431) | copy-start | bytes 1966084
  116.5 7.2 %copy-start.14 = (f32[2,5,64,256]{3,2,1,0:T(8,128)}, f32[2,5,64,256]{3,2,1,0:T(8,128)S(1)}, u32[]{:S(2)}) copy-start(f32[2,5,64,256]{3,2,1,0:T(8,128)S(1)} %copy.430) | copy-start | bytes 1966084
  118.5 5.2 %copy-start.16 = (f32[2,5,64,256]{3,2,1,0:T(8,128)}, f32[2,5,64,256]{3,2,1,0:T(8,128)S(1)}, u32[]{:S(2)}) copy-start(f32[2,5,64,256]{3,2,1,0:T(8,128)S(1)} %copy.429) | copy-start | bytes 1966084
  121.3 2.4 %copy-start.18 = (f32[2,5,64,256]{3,2,1,0:T(8,128)S(1)}, f32[2,5,64,256]{3,2,1,0:T(8,128)}, u32[]{:S(2)}) copy-start(f32[2,5,64,256]{3,2,1,0:T(8,128)} %copy.428) | copy-start | bytes 1966084
  126.0 13.7 %copy-start.31 = (s32[2,5]{1,0:T(2,128)S(1)}, s32[2,5]{1,0:T(2,128)}, u32[]{:S(2)}) copy-start(s32[2,5]{1,0:T(2,128)} %param.21) | copy-start | bytes 124
  127.2 14.0 %copy-start.3 = (f32[2,5,64,256]{3,2,1,0:T(8,128)S(1)}, f32[2,5,64,256]{3,2,1,0:T(8,128)}, u32[]{:S(2)}) copy-start(f32[2,5,64,256]{3,2,1,0:T(8,128)} %copy.436) | copy-start | bytes 1966084
  127.2 14.0 %copy-start.5 = (f32[2,5,64,256]{3,2,1,0:T(8,128)S(1)}, f32[2,5,64,256]{3,2,1,0:T(8,128)}, u32[]{:S(2)}) copy-start(f32[2,5,64,256]{3,2,1,0:T(8,128)} %copy.435) | copy-start | bytes 1966084
  127.2 14.0 %copy-start.7 = (f32[2,5,64,256]{3,2,1,0:T(8,128)S(1)}, f32[2,5,64,256]{3,2,1,0:T(8,128)}, u32[]{:S(2)}) copy-start(f32[2,5,64,256]{3,2,1,0:T(8,128)} %copy.434) | copy-start | bytes 1966084
  127.2 14.0 %copy-start.9 = (f32[2,5,64,256]{3,2,1,0:T(8,128)S(1)}, f32[2,5,64,256]{3,2,1,0:T(8,128)}, u32[]{:S(2)}) copy-start(f32[2,5,64,256]{3,2,1,0:T(8,128)} %copy.433) | copy-start | bytes 1966084
  129.3 11.8 %collective-permute-start.8 = (f32[2,2,64,256]{3,2,1,0:T(8,128)}, f32[2,2,64,256]{3,2,1,0:T(8,128)}, u32[]{:S(2)}, u32[]{:S(2)}) collective-permute-start(f32[2,2,64,256]{3,2,1,0:T(8,128)} %get-tuple-element.62), channel_id=1, source_target_pairs={{0,8},{8,16},{16,24},{24,32},{32,40},{40,48},{48,56},{56,64},{64,7... | collective-permute-start | bytes 786440 | tf_op jit(solution)/shard_map/ppermute | solution.py:19
  129.3 16.9 %collective-permute-start.9 = (f32[2,2,64,256]{3,2,1,0:T(8,128)}, f32[2,2,64,256]{3,2,1,0:T(8,128)S(1)}, u32[]{:S(2)}, u32[]{:S(2)}) collective-permute-start(f32[2,2,64,256]{3,2,1,0:T(8,128)} %get-tuple-element.61), channel_id=1, source_target_pairs={{8,0},{16,8},{24,16},{32,24},{40,32},{48,40},{56,48},{64,56},{72,6... | collective-permute-start | bytes 786440 | tf_op jit(solution)/shard_map/ppermute | solution.py:21
  134.1 11.1 %collective-permute-start.6 = (f32[2,2,64,256]{3,2,1,0:T(8,128)}, f32[2,2,64,256]{3,2,1,0:T(8,128)}, u32[]{:S(2)}, u32[]{:S(2)}) collective-permute-start(f32[2,2,64,256]{3,2,1,0:T(8,128)} %get-tuple-element.64), channel_id=1, source_target_pairs={{0,8},{8,16},{16,24},{24,32},{32,40},{40,48},{48,56},{56,64},{64,7... | collective-permute-start | bytes 786440 | tf_op jit(solution)/shard_map/ppermute | solution.py:19
  134.1 12.2 %collective-permute-start.7 = (f32[2,2,64,256]{3,2,1,0:T(8,128)}, f32[2,2,64,256]{3,2,1,0:T(8,128)}, u32[]{:S(2)}, u32[]{:S(2)}) collective-permute-start(f32[2,2,64,256]{3,2,1,0:T(8,128)} %get-tuple-element.63), channel_id=1, source_target_pairs={{8,0},{16,8},{24,16},{32,24},{40,32},{48,40},{56,48},{64,56},{72,6... | collective-permute-start | bytes 786440 | tf_op jit(solution)/shard_map/ppermute | solution.py:21
  139.7 5.5 %slice-start = ((f32[2,9,64,256]{3,2,1,0:T(8,128)}), f32[2,5,64,256]{3,2,1,0:T(8,128)S(1)}, s32[]{:S(2)}) async-start(f32[2,9,64,256]{3,2,1,0:T(8,128)} %pad_add_fusion.1), calls=%async_computation.3 | async-start | bytes 1310720 | tf_op jit(solution)/shard_map/slice | solution.py:213
  141.1 4.1 %copy-start.11 = (f32[2,5,64,256]{3,2,1,0:T(8,128)S(1)}, f32[2,5,64,256]{3,2,1,0:T(8,128)}, u32[]{:S(2)}) copy-start(f32[2,5,64,256]{3,2,1,0:T(8,128)} %copy-done.10) | copy-start | bytes 1966084
  141.1 4.1 %copy-start.13 = (f32[2,5,64,256]{3,2,1,0:T(8,128)S(1)}, f32[2,5,64,256]{3,2,1,0:T(8,128)}, u32[]{:S(2)}) copy-start(f32[2,5,64,256]{3,2,1,0:T(8,128)} %copy-done.12) | copy-start | bytes 1966084
  141.1 4.1 %copy-start.15 = (f32[2,5,64,256]{3,2,1,0:T(8,128)S(1)}, f32[2,5,64,256]{3,2,1,0:T(8,128)}, u32[]{:S(2)}) copy-start(f32[2,5,64,256]{3,2,1,0:T(8,128)} %copy-done.14) | copy-start | bytes 1966084
  141.1 4.1 %copy-start.17 = (f32[2,5,64,256]{3,2,1,0:T(8,128)S(1)}, f32[2,5,64,256]{3,2,1,0:T(8,128)}, u32[]{:S(2)}) copy-start(f32[2,5,64,256]{3,2,1,0:T(8,128)} %copy-done.16) | copy-start | bytes 1966084
  141.1 4.1 %copy-start.19 = (f32[2,5,64,256]{3,2,1,0:T(8,128)S(1)}, f32[2,5,64,256]{3,2,1,0:T(8,128)}, u32[]{:S(2)}) copy-start(f32[2,5,64,256]{3,2,1,0:T(8,128)} %copy.428) | copy-start | bytes 1966084
  143.1 3.2 %copy-start.26 = (f32[2,5,64,256]{3,2,1,0:T(8,128)S(1)}, f32[2,5,64,256]{3,2,1,0:T(8,128)}, u32[]{:S(2)}) copy-start(f32[2,5,64,256]{3,2,1,0:T(8,128)} %fusion.36) | copy-start | bytes 1966084
Sparse Core Ops, SparseCore 0:
  106.4 12.8 reduce-scatter.3
